TPU v7x, 256 devices: a whole 4x4x8 slice. The times are simulated.
256 devices in a mesh: lvl: 4 (over y), cell: 64 (over x, z, core).
Axes of the slice: x: 4, y: 4, z: 8, core: 2. Of those that a mesh axis runs over, the one named last changes fastest.
Arguments:
- rhs: float32 [16, 1024, 1024], P('lvl', 'cell'), may hold values from -6 to 6
- adjoint_owned: float32 [16, 1024, 1024], P('lvl', 'cell'), may hold values from -6 to 6
- owner_of: int32 [16, 1024], P('lvl', 'cell'), may hold values from 0 to 16383, as said below
- columns: int32 [16, 1024, 3], P('lvl', 'cell'), may hold values from 0 to 1023, as said below
- lower: float32 [16, 1024, 3, 4096], P('lvl', 'cell'), may hold values from -0.4375 to 0.4375
- dinv: float32 [16, 1024, 4096], P('lvl', 'cell'), may hold values from -0.3 to 1, as said below
Outputs:
- solved: float32 [16, 1024, 1024], P('lvl', 'cell')
- adjoint: float32 [16, 1024, 1024], P('lvl', 'cell')
Inputs may be any that keep to these rules, and one draw needn't show every extreme that they name: `columns`: entry k of block row q of level l names a row of level l - 1 whose position differs from q by at most 8 cyclically over 1024 rows; the 3 entries of a row differ. `owner_of`: A permutation that keeps each section of 4 consecutive levels within itself. Numbering a device's owner positions m = (level mod 4) * 16 + (row mod 16), the block row q of level order sits at an owner position whose m, modulo the number of devices along cell, equals q // 16. `dinv`: diagonal entries of each block between 0.6 and 1.
All inputs are finite; a program needn't handle non-finite values.
Results may differ from a plain program's by a relative error of at most 0.00011.
Values sent between devices are 32-bit elements; how exact they have to be, the bound alone decides.
No kernel may reach another device: no remote copies, remote signals or barrier semaphores. Data moves between devices by JAX's collectives and lax.ppermute only.
A program may use at most 192 MiB of HBM per device.

v0:
```python
from functools import partial

import jax
import jax.numpy as jnp
from jax import lax
from jax.sharding import PartitionSpec as P

B = 64
K = 3
W = 8


def from_behind(array, axis, by):
    peers = lax.axis_size(axis)
    pairs = [(i, i + by) for i in range(peers) if 0 <= i + by < peers]
    return lax.ppermute(array, axis, pairs)


def with_halo(array, sides, width):
    for axis, dim in sides:
        peers, length = (lax.axis_size(axis), array.shape[dim])
        up = [(i, (i + 1) % peers) for i in range(peers)]
        down = [(j, i) for i, j in up]
        last = lax.slice_in_dim(array, length - width, length, axis=dim)
        initial = lax.slice_in_dim(array, 0, width, axis=dim)
        before = lax.ppermute(last, axis, up)
        after = lax.ppermute(initial, axis, down)
        array = jnp.concatenate([before, array, after], axis=dim)
    return array


def per_device(rhs, adjoint_owned, owner_of, columns, lower, dinv):
    highest = lax.Precision.HIGHEST
    level_count, row_count, feat_width = rhs.shape
    vec_count = feat_width // B
    cell_count = lax.axis_size("cell")
    section_count = lax.axis_size("lvl")
    cell_index = lax.axis_index("cell")
    section_index = lax.axis_index("lvl")
    span_rows = row_count * cell_count
    positions = cell_index * row_count + jnp.arange(row_count, dtype=jnp.int32)
    offsets = (columns - positions[None, :, None] + span_rows // 2) % span_rows - span_rows // 2
    ext_index = jnp.arange(row_count, dtype=jnp.int32)[None, :, None] + W + offsets
    owned_rows = adjoint_owned.reshape(
        level_count * row_count // cell_count, cell_count, feat_width
    )
    relayed = lax.all_to_all(owned_rows, "cell", split_axis=1, concat_axis=1, tiled=True).reshape(
        level_count * row_count, feat_width
    )
    owner_level = owner_of // span_rows
    owner_row = owner_of % span_rows
    owner_cell = owner_row // row_count
    owner_local = owner_level % level_count * row_count + owner_row % row_count
    take_index = owner_local // cell_count * cell_count + owner_cell
    adjoint_level = jnp.take(relayed, take_index.reshape(-1), axis=0).reshape(
        level_count, row_count, feat_width
    )
    group_count = 1
    stretch_vec = vec_count // group_count
    stretch_width = B * stretch_vec
    round_count = section_count + group_count - 1
    rhs_groups = rhs.reshape(level_count, row_count, B, group_count, stretch_vec)
    adjoint_groups = adjoint_level.reshape(level_count, row_count, B, group_count, stretch_vec)

    def select_group(groups):
        return groups.reshape(level_count, row_count, stretch_width)

    def place_group(groups, values, live):
        update = jnp.where(live, values.reshape(level_count, row_count, B, 1, stretch_vec), groups)
        return update

    def forward_local(level_idx, source, prev_ext):
        gathered = jnp.take(prev_ext, ext_index[level_idx].reshape(-1), axis=0).reshape(
            row_count, K, B, stretch_vec
        )
        blocks = lower[level_idx].reshape(row_count, K, B, B)
        coupled = jnp.einsum("rkab,rkbv->rav", blocks, gathered, precision=highest)
        remain = source.reshape(row_count, B, stretch_vec) - coupled
        inverse = dinv[level_idx].reshape(row_count, B, B)
        return jnp.einsum("rab,rbv->rav", inverse, remain, precision=highest).reshape(
            row_count, stretch_width
        )

    def backward_local(level_idx, source, pending):
        inverse = dinv[level_idx].reshape(row_count, B, B)
        remain = source.reshape(row_count, B, stretch_vec) - pending.reshape(
            row_count, B, stretch_vec
        )
        result = jnp.einsum("rba,rbv->rav", inverse, remain, precision=highest)
        blocks = lower[level_idx].reshape(row_count, K, B, B)
        spread = jnp.einsum("rkba,rbv->rkav", blocks, result, precision=highest).reshape(
            row_count * K, stretch_width
        )
        extended = (
            jnp.zeros((row_count + 2 * W, stretch_width), jnp.float32)
            .at[ext_index[level_idx].reshape(-1)]
            .add(spread)
        )
        return (result.reshape(row_count, stretch_width), extended)

    filler = jnp.zeros((row_count - 2 * W, stretch_width), jnp.float32)

    def guarded(segment_live, compute, operand, spare_value):
        return lax.cond(segment_live, compute, lambda unused: spare_value, operand)

    def live_group(group_idx):
        return jnp.logical_and(group_idx >= 0, group_idx < group_count)

    zero_rows = jnp.zeros((row_count, stretch_width), jnp.float32)
    zero_ext = jnp.zeros((row_count + 2 * W, stretch_width), jnp.float32)
    solved_groups = jnp.zeros((level_count, row_count, B, group_count, stretch_vec), jnp.float32)
    adjoint_out = jnp.zeros((level_count, row_count, B, group_count, stretch_vec), jnp.float32)
    incoming = zero_rows
    for round_idx in range(round_count):
        forward_group = round_idx - section_index
        forward_live = live_group(forward_group)
        forward_src = select_group(rhs_groups)
        forward_out = [None] * level_count
        previous = incoming
        for level_idx in range(level_count):
            received = with_halo(previous, (("cell", 0),), W)
            previous = guarded(
                forward_live,
                partial(forward_local, level_idx, forward_src[level_idx]),
                received,
                zero_rows,
            )
            forward_out[level_idx] = previous
        solved_groups = place_group(solved_groups, jnp.stack(forward_out), forward_live)
        if round_idx + 1 < round_count:
            incoming = from_behind(previous, "lvl", 1)
    carried = zero_ext
    for round_idx in range(round_count):
        backward_group = round_idx - (section_count - 1 - section_index)
        backward_live = live_group(backward_group)
        backward_src = select_group(adjoint_groups)
        backward_out = [None] * level_count
        extended = carried
        for level_idx in range(level_count):
            upper_idx = level_count - 1 - level_idx
            received = with_halo(
                jnp.concatenate([extended[:W], filler, extended[row_count + W :]], axis=0),
                (("cell", 0),),
                W,
            )
            pending = extended[W : row_count + W] + jnp.concatenate(
                [received[:W], filler, received[row_count + W :]], axis=0
            )
            result, extended = guarded(
                backward_live,
                partial(backward_local, upper_idx, backward_src[upper_idx]),
                pending,
                (zero_rows, zero_ext),
            )
            backward_out[upper_idx] = result
        adjoint_out = place_group(adjoint_out, jnp.stack(backward_out), backward_live)
        if round_idx + 1 < round_count:
            carried = from_behind(extended, "lvl", -1)
    solved_all = solved_groups.reshape(level_count, row_count, feat_width)
    adjoint_all = adjoint_out.reshape(level_count, row_count, feat_width)
    return (solved_all, adjoint_all)


def solution(mesh):
    return jax.shard_map(
        per_device,
        mesh=mesh,
        in_specs=(
            P("lvl", "cell", None),
            P("lvl", "cell", None),
            P("lvl", "cell"),
            P("lvl", "cell", None),
            P("lvl", "cell", None, None),
            P("lvl", "cell", None),
        ),
        out_specs=(P("lvl", "cell", None), P("lvl", "cell", None)),
        check_vma=False,
    )
```

profile of v0, /device:TPU:0, one launch (start us, length us, event | category | flops | bytes accessed | tf_op | source)
XLA Modules:
  0.0 765.1 jit_solution(12060269898488051527)
XLA Ops:
  0.6 5.8 collective-permute-start.1
  13.7 14.0 %conditional.32 = (f32[16,1024]{1,0:T(8,128)S(1)}) conditional(s32[]{:T(128)} %convert_element_type.19, () %tuple.289, (f32[1,16,1024]{2,1,0:T(8,128)S(1)}, s32[4,16,3]{2,1,0:T(8,128)S(1)}, f32[32,1024]{1,0:T(8,128)S(1)}, f32[4,16,3,4096]{3,1,2,0:T(8,128)}, f32[4,16,4096]{2,1,0:T(8,128)}) %tuple.290), branch_computations={%region_0.1_spmd, %region_1.3_spmd} | conditional | flops 50398640 | bytes 7411496 | solution.py:104
  29.9 5.1 collective-permute-done.2
  34.9 15.1 %conditional.33 = (f32[16,1024]{1,0:T(8,128)}) conditional(s32[]{:T(128)} %convert_element_type.19, () %tuple.288, (f32[1,16,1024]{2,1,0:T(8,128)S(1)}, s32[4,16,3]{2,1,0:T(8,128)S(1)}, f32[32,1024]{1,0:T(8,128)S(1)}, f32[4,16,3,4096]{3,1,2,0:T(8,128)}, f32[4,16,4096]{2,1,0:T(8,128)}) %tuple.291), branch_computations={%region_2.4_spmd, %region_3.5_spmd} | conditional | flops 50398640 | bytes 7411496 | solution.py:104
  53.3 7.2 all-to-all-start
  61.4 14.2 %conditional.34 = (f32[16,1024]{1,0:T(8,128)S(1)}) conditional(s32[]{:T(128)} %convert_element_type.19, () %tuple.287, (f32[1,16,1024]{2,1,0:T(8,128)S(1)}, s32[4,16,3]{2,1,0:T(8,128)S(1)}, f32[32,1024]{1,0:T(8,128)S(1)}, f32[4,16,3,4096]{3,1,2,0:T(8,128)}, f32[4,16,4096]{2,1,0:T(8,128)}) %tuple.292), branch_computations={%region_4.6_spmd, %region_5.7_spmd} | conditional | flops 50398640 | bytes 7411496 | solution.py:104
  82.1 5.1 collective-permute-done.6
  87.2 15.8 %conditional.35 = (f32[16,1024]{1,0:T(8,128)}, f32[1,16,1024]{2,1,0:T(8,128)}) conditional(s32[]{:T(128)} %convert_element_type.19, () %tuple.286, (f32[1,16,1024]{2,1,0:T(8,128)S(1)}, s32[4,16,3]{2,1,0:T(8,128)S(1)}, f32[32,1024]{1,0:T(8,128)S(1)}, f32[4,16,3,4096]{3,1,2,0:T(8,128)}, f32[4,16,4096]{2,1,0:T(8,128)}) %tuple.293), branch_computations={%region_6.8_spmd, %region_7.9_spmd} | conditional | flops 50398640 | bytes 7542576 | solution.py:104
  108.1 5.1 collective-permute-done.9
  115.2 5.1 collective-permute-done.11
  133.1 6.8 conditional.48
  148.1 70.4 %collective-permute-start.17 = (f32[16,1024]{1,0:T(8,128)}, f32[16,1024]{1,0:T(8,128)}, u32[]{:S(2)}, u32[]{:S(2)}) collective-permute-start(f32[16,1024]{1,0:T(8,128)} %get-tuple-element.579), channel_id=1, source_target_pairs={{0,64},{64,128},{128,192},{1,65},{65,129},{129,193},{2,66},{66,130... | collective-permute-start | bytes 196616 | tf_op jit(solution)/shard_map/ppermute | solution.py:16
  219.3 8.8 %conditional.49 = (f32[32,1024]{1,0:T(8,128)}, f32[1,16,1024]{2,1,0:T(8,128)}) conditional(s32[]{:T(128)} %convert_element_type.23, () %tuple.323, (s32[4,16,3]{2,1,0:T(8,128)S(1)}, f32[1,16,1024]{2,1,0:T(8,128)}, f32[32,1024]{1,0:T(8,128)}, f32[4,16,4096]{2,1,0:T(8,128)}, f32[4,16,3,4096]{3,1,2,0:T(8,128)S(1)}, ...), branch_computations={%region_35.37_spmd, %region_36.39_spmd} | conditional | flops 50413712 | bytes 10749640 | solution.py:104
  235.1 5.1 collective-permute-start.19
  249.3 5.1 collective-permute-done.39
  266.4 5.1 collective-permute-done.42
  291.1 5.1 collective-permute-done.46
  299.0 5.6 collective-permute-start.48
  320.0 12.6 %collective-permute-start.26 = (f32[16,1024]{1,0:T(8,128)}, f32[16,1024]{1,0:T(8,128)S(1)}, u32[]{:S(2)}, u32[]{:S(2)}) collective-permute-start(f32[16,1024]{1,0:T(8,128)} %get-tuple-element.580), channel_id=1, source_target_pairs={{0,64},{64,128},{128,192},{1,65},{65,129},{129,193},{2,66},{66,130... | collective-permute-start | bytes 196616 | tf_op jit(solution)/shard_map/ppermute | solution.py:16
  350.3 5.1 collective-permute-done.53
  384.7 274.5 %collective-permute-done.59 = f32[32,1024]{1,0:T(8,128)S(1)} collective-permute-done((f32[32,1024]{1,0:T(8,128)}, f32[32,1024]{1,0:T(8,128)S(1)}, u32[]{:S(2)}, u32[]{:S(2)}) %collective-permute-start.59) | collective-permute-done | bytes 131104 | tf_op jit(solution)/shard_map/ppermute | solution.py:16
  667.6 26.2 %conditional.60 = (f32[32,1024]{1,0:T(8,128)}, f32[1,16,1024]{2,1,0:T(8,128)S(1)}) conditional(s32[]{:T(128)} %convert_element_type.20, () %tuple.312, (s32[4,16,3]{2,1,0:T(8,128)S(1)}, f32[1,16,1024]{2,1,0:T(8,128)}, f32[32,1024]{1,0:T(8,128)}, f32[4,16,4096]{2,1,0:T(8,128)}, f32[4,16,3,4096]{3,1,2,0:T(8,128)S(1)}, ...), branch_computations={%region_68.70_spmd, %region_69.72_spmd} | conditional | flops 50413712 | bytes 10487468 | solution.py:104
  701.3 24.9 %conditional.61 = (f32[32,1024]{1,0:T(8,128)}, f32[1,16,1024]{2,1,0:T(8,128)S(1)}) conditional(s32[]{:T(128)} %convert_element_type.20, () %tuple.311, (s32[4,16,3]{2,1,0:T(8,128)S(1)}, f32[1,16,1024]{2,1,0:T(8,128)S(1)}, f32[32,1024]{1,0:T(8,128)}, f32[4,16,4096]{2,1,0:T(8,128)}, f32[4,16,3,4096]{3,1,2,0:T(8,128)S(1)}, ...), branch_computations={%region_71.73_spmd, %region_72.75_spmd} | conditional | flops 50413712 | bytes 10487468 | solution.py:104
  739.6 11.6 %conditional.62 = (f32[32,1024]{1,0:T(8,128)}, f32[1,16,1024]{2,1,0:T(8,128)}) conditional(s32[]{:T(128)} %convert_element_type.20, () %tuple.310, (s32[4,16,3]{2,1,0:T(8,128)S(1)}, f32[1,16,1024]{2,1,0:T(8,128)S(1)}, f32[32,1024]{1,0:T(8,128)}, f32[4,16,4096]{2,1,0:T(8,128)}, f32[4,16,3,4096]{3,1,2,0:T(8,128)S(1)}, ...), branch_computations={%region_74.76_spmd, %region_75.78_spmd} | conditional | flops 50413712 | bytes 7341204 | solution.py:104
  (494 shorter events, 343.7 us)
Async XLA Ops:
  50.8 9.7 %collective-permute-start.5 = (f32[8,1024]{1,0:T(8,128)S(1)}, f32[8,1024]{1,0:T(8,128)S(1)}, u32[]{:S(2)}, u32[]{:S(2)}) collective-permute-start(f32[8,1024]{1,0:T(8,128)S(1)} %get-tuple-element.893), channel_id=1, source_target_pairs={{1,0},{2,1},{3,2},{4,3},{5,4},{6,5},{7,6},{8,7},{9,8},{10,9},{11,1... | collective-permute-start | bytes 98312 | tf_op jit(solution)/shard_map/ppermute | solution.py:27
  50.8 9.7 %collective-permute-start.4 = (f32[8,1024]{1,0:T(8,128)S(1)}, f32[8,1024]{1,0:T(8,128)S(1)}, u32[]{:S(2)}, u32[]{:S(2)}) collective-permute-start(f32[8,1024]{1,0:T(8,128)S(1)} %get-tuple-element.892), channel_id=1, source_target_pairs={{0,1},{1,2},{2,3},{3,4},{4,5},{5,6},{6,7},{7,8},{8,9},{9,10},{10,1... | collective-permute-start | bytes 98312 | tf_op jit(solution)/shard_map/ppermute | solution.py:26
  53.3 75.7 %all-to-all-start = ((f32[1,64,1024]{2,0,1:T(1,128)}), f32[1,64,1024]{2,0,1:T(1,128)}, u32[]{:S(2)}, u32[]{:S(2)}) async-start(f32[1,64,1024]{2,0,1:T(1,128)} %reshape.969), calls=%async_computation | async-start | bytes 524288 | tf_op jit(solution)/shard_map/all_to_all | solution.py:47
  128.5 17.4 %collective-permute-start.16 = (f32[8,1024]{1,0:T(8,128)}, f32[8,1024]{1,0:T(8,128)}, u32[]{:S(2)}, u32[]{:S(2)}) collective-permute-start(f32[8,1024]{1,0:T(8,128)} %get-tuple-element.883), channel_id=1, source_target_pairs={{1,0},{2,1},{3,2},{4,3},{5,4},{6,5},{7,6},{8,7},{9,8},{10,9},{11,1... | collective-permute-start | bytes 98312 | tf_op jit(solution)/shard_map/ppermute | solution.py:27
  128.5 17.4 %collective-permute-start.15 = (f32[8,1024]{1,0:T(8,128)S(1)}, f32[8,1024]{1,0:T(8,128)}, u32[]{:S(2)}, u32[]{:S(2)}) collective-permute-start(f32[8,1024]{1,0:T(8,128)S(1)} %get-tuple-element.882), channel_id=1, source_target_pairs={{0,1},{1,2},{2,3},{3,4},{4,5},{5,6},{6,7},{7,8},{8,9},{9,10},{10,1... | collective-permute-start | bytes 98312 | tf_op jit(solution)/shard_map/ppermute | solution.py:26
  141.3 77.2 %collective-permute-start.36 = (f32[8,1024]{1,0:T(8,128)}, f32[8,1024]{1,0:T(8,128)}, u32[]{:S(2)}, u32[]{:S(2)}) collective-permute-start(f32[8,1024]{1,0:T(8,128)} %get-tuple-element.865), channel_id=1, source_target_pairs={{1,0},{2,1},{3,2},{4,3},{5,4},{6,5},{7,6},{8,7},{9,8},{10,9},{11,1... | collective-permute-start | bytes 98312 | tf_op jit(solution)/shard_map/ppermute | solution.py:27
  145.9 72.6 %collective-permute-start.35 = (f32[8,1024]{1,0:T(8,128)}, f32[8,1024]{1,0:T(8,128)}, u32[]{:S(2)}, u32[]{:S(2)}) collective-permute-start(f32[8,1024]{1,0:T(8,128)} %get-tuple-element.864), channel_id=1, source_target_pairs={{0,1},{1,2},{2,3},{3,4},{4,5},{5,6},{6,7},{7,8},{8,9},{9,10},{10,1... | collective-permute-start | bytes 98312 | tf_op jit(solution)/shard_map/ppermute | solution.py:26
  148.1 85.6 %collective-permute-start.17 = (f32[16,1024]{1,0:T(8,128)}, f32[16,1024]{1,0:T(8,128)}, u32[]{:S(2)}, u32[]{:S(2)}) collective-permute-start(f32[16,1024]{1,0:T(8,128)} %get-tuple-element.579), channel_id=1, source_target_pairs={{0,64},{64,128},{128,192},{1,65},{65,129},{129,193},{2,66},{66,130... | collective-permute-start | bytes 196616 | tf_op jit(solution)/shard_map/ppermute | solution.py:16
  228.9 11.2 %collective-permute-start.38 = (f32[8,1024]{1,0:T(8,128)S(1)}, f32[8,1024]{1,0:T(8,128)S(1)}, u32[]{:S(2)}, u32[]{:S(2)}) collective-permute-start(f32[8,1024]{1,0:T(8,128)S(1)} %get-tuple-element.863), channel_id=1, source_target_pairs={{1,0},{2,1},{3,2},{4,3},{5,4},{6,5},{7,6},{8,7},{9,8},{10,9},{11,1... | collective-permute-start | bytes 98312 | tf_op jit(solution)/shard_map/ppermute | solution.py:27
  235.1 12.3 %collective-permute-start.19 = (f32[8,1024]{1,0:T(8,128)}, f32[8,1024]{1,0:T(8,128)}, u32[]{:S(2)}, u32[]{:S(2)}) collective-permute-start(f32[8,1024]{1,0:T(8,128)} %get-tuple-element.881), channel_id=1, source_target_pairs={{1,0},{2,1},{3,2},{4,3},{5,4},{6,5},{7,6},{8,7},{9,8},{10,9},{11,1... | collective-permute-start | bytes 98312 | tf_op jit(solution)/shard_map/ppermute | solution.py:27
  276.7 12.5 %collective-permute-start.23 = (f32[8,1024]{1,0:T(8,128)}, f32[8,1024]{1,0:T(8,128)}, u32[]{:S(2)}, u32[]{:S(2)}) collective-permute-start(f32[8,1024]{1,0:T(8,128)} %get-tuple-element.877), channel_id=1, source_target_pairs={{1,0},{2,1},{3,2},{4,3},{5,4},{6,5},{7,6},{8,7},{9,8},{10,9},{11,1... | collective-permute-start | bytes 98312 | tf_op jit(solution)/shard_map/ppermute | solution.py:27
  299.0 12.1 %collective-permute-start.49 = (f32[8,1024]{1,0:T(8,128)S(1)}, f32[8,1024]{1,0:T(8,128)S(1)}, u32[]{:S(2)}, u32[]{:S(2)}) collective-permute-start(f32[8,1024]{1,0:T(8,128)S(1)} %get-tuple-element.853), channel_id=1, source_target_pairs={{1,0},{2,1},{3,2},{4,3},{5,4},{6,5},{7,6},{8,7},{9,8},{10,9},{11,1... | collective-permute-start | bytes 98312 | tf_op jit(solution)/shard_map/ppermute | solution.py:27
  299.0 12.3 %collective-permute-start.48 = (f32[8,1024]{1,0:T(8,128)S(1)}, f32[8,1024]{1,0:T(8,128)S(1)}, u32[]{:S(2)}, u32[]{:S(2)}) collective-permute-start(f32[8,1024]{1,0:T(8,128)S(1)} %get-tuple-element.852), channel_id=1, source_target_pairs={{0,1},{1,2},{2,3},{3,4},{4,5},{5,6},{6,7},{7,8},{8,9},{9,10},{10,1... | collective-permute-start | bytes 98312 | tf_op jit(solution)/shard_map/ppermute | solution.py:26
  306.0 7.9 %collective-permute-start.25 = (f32[8,1024]{1,0:T(8,128)}, f32[8,1024]{1,0:T(8,128)}, u32[]{:S(2)}, u32[]{:S(2)}) collective-permute-start(f32[8,1024]{1,0:T(8,128)} %get-tuple-element.875), channel_id=1, source_target_pairs={{1,0},{2,1},{3,2},{4,3},{5,4},{6,5},{7,6},{8,7},{9,8},{10,9},{11,1... | collective-permute-start | bytes 98312 | tf_op jit(solution)/shard_map/ppermute | solution.py:27
  312.6 20.0 %collective-permute-start.50 = (f32[32,1024]{1,0:T(8,128)}, f32[32,1024]{1,0:T(8,128)}, u32[]{:S(2)}, u32[]{:S(2)}) collective-permute-start(f32[32,1024]{1,0:T(8,128)} %get-tuple-element.591), channel_id=1, source_target_pairs={{64,0},{128,64},{192,128},{65,1},{129,65},{193,129},{66,2},{130,66... | collective-permute-start | bytes 393224 | tf_op jit(solution)/shard_map/ppermute | solution.py:16
  320.0 14.8 %collective-permute-start.26 = (f32[16,1024]{1,0:T(8,128)}, f32[16,1024]{1,0:T(8,128)S(1)}, u32[]{:S(2)}, u32[]{:S(2)}) collective-permute-start(f32[16,1024]{1,0:T(8,128)} %get-tuple-element.580), channel_id=1, source_target_pairs={{0,64},{64,128},{128,192},{1,65},{65,129},{129,193},{2,66},{66,130... | collective-permute-start | bytes 196616 | tf_op jit(solution)/shard_map/ppermute | solution.py:16
  335.4 13.0 %collective-permute-start.28 = (f32[8,1024]{1,0:T(8,128)}, f32[8,1024]{1,0:T(8,128)}, u32[]{:S(2)}, u32[]{:S(2)}) collective-permute-start(f32[8,1024]{1,0:T(8,128)} %get-tuple-element.873), channel_id=1, source_target_pairs={{1,0},{2,1},{3,2},{4,3},{5,4},{6,5},{7,6},{8,7},{9,8},{10,9},{11,1... | collective-permute-start | bytes 98312 | tf_op jit(solution)/shard_map/ppermute | solution.py:27
  340.4 8.0 %collective-permute-start.27 = (f32[8,1024]{1,0:T(8,128)S(1)}, f32[8,1024]{1,0:T(8,128)}, u32[]{:S(2)}, u32[]{:S(2)}) collective-permute-start(f32[8,1024]{1,0:T(8,128)S(1)} %get-tuple-element.872), channel_id=1, source_target_pairs={{0,1},{1,2},{2,3},{3,4},{4,5},{5,6},{6,7},{7,8},{8,9},{9,10},{10,1... | collective-permute-start | bytes 98312 | tf_op jit(solution)/shard_map/ppermute | solution.py:26
  360.4 12.5 %collective-permute-start.30 = (f32[8,1024]{1,0:T(8,128)}, f32[8,1024]{1,0:T(8,128)}, u32[]{:S(2)}, u32[]{:S(2)}) collective-permute-start(f32[8,1024]{1,0:T(8,128)} %get-tuple-element.871), channel_id=1, source_target_pairs={{1,0},{2,1},{3,2},{4,3},{5,4},{6,5},{7,6},{8,7},{9,8},{10,9},{11,1... | collective-permute-start | bytes 98312 | tf_op jit(solution)/shard_map/ppermute | solution.py:27
  381.9 277.2 %collective-permute-start.59 = (f32[32,1024]{1,0:T(8,128)}, f32[32,1024]{1,0:T(8,128)S(1)}, u32[]{:S(2)}, u32[]{:S(2)}) collective-permute-start(f32[32,1024]{1,0:T(8,128)} %get-tuple-element.595), channel_id=1, source_target_pairs={{64,0},{128,64},{192,128},{65,1},{129,65},{193,129},{66,2},{130,66... | collective-permute-start | bytes 393224 | tf_op jit(solution)/shard_map/ppermute | solution.py:16
  384.0 276.3 %collective-permute-start.32 = (f32[8,1024]{1,0:T(8,128)S(1)}, f32[8,1024]{1,0:T(8,128)S(1)}, u32[]{:S(2)}, u32[]{:S(2)}) collective-permute-start(f32[8,1024]{1,0:T(8,128)S(1)} %get-tuple-element.869), channel_id=1, source_target_pairs={{1,0},{2,1},{3,2},{4,3},{5,4},{6,5},{7,6},{8,7},{9,8},{10,9},{11,1... | collective-permute-start | bytes 98312 | tf_op jit(solution)/shard_map/ppermute | solution.py:27
  384.0 276.3 %collective-permute-start.31 = (f32[8,1024]{1,0:T(8,128)S(1)}, f32[8,1024]{1,0:T(8,128)S(1)}, u32[]{:S(2)}, u32[]{:S(2)}) collective-permute-start(f32[8,1024]{1,0:T(8,128)S(1)} %get-tuple-element.868), channel_id=1, source_target_pairs={{0,1},{1,2},{2,3},{3,4},{4,5},{5,6},{6,7},{7,8},{8,9},{9,10},{10,1... | collective-permute-start | bytes 98312 | tf_op jit(solution)/shard_map/ppermute | solution.py:26
  695.7 36.1 %collective-permute-start.34 = (f32[8,1024]{1,0:T(8,128)}, f32[8,1024]{1,0:T(8,128)}, u32[]{:S(2)}, u32[]{:S(2)}) collective-permute-start(f32[8,1024]{1,0:T(8,128)} %get-tuple-element.867), channel_id=1, source_target_pairs={{1,0},{2,1},{3,2},{4,3},{5,4},{6,5},{7,6},{8,7},{9,8},{10,9},{11,1... | collective-permute-start | bytes 98312 | tf_op jit(solution)/shard_map/ppermute | solution.py:27
  700.3 31.5 %collective-permute-start.33 = (f32[8,1024]{1,0:T(8,128)S(1)}, f32[8,1024]{1,0:T(8,128)}, u32[]{:S(2)}, u32[]{:S(2)}) collective-permute-start(f32[8,1024]{1,0:T(8,128)S(1)} %get-tuple-element.866), channel_id=1, source_target_pairs={{0,1},{1,2},{2,3},{3,4},{4,5},{5,6},{6,7},{7,8},{8,9},{9,10},{10,1... | collective-permute-start | bytes 98312 | tf_op jit(solution)/shard_map/ppermute | solution.py:26
  (93 other events, 1185.2 us)
where the time goes:
time: 777 us; the launch traced here: 765 us
  waiting for transfers between devices  368 us (47%)
  starting transfers between devices  183 us (24%)
  local copies, waits for them, and re-layouts  128 us (16%)
  matrix products  35.7 us (5%)
  other arithmetic  32.6 us (4%)
  loops' own time  17.1 us (2%)
    ppermute x6, waiting for transfers between devices, from_behind(): return lax.ppermute(array, axis, pairs)  281 us
    ppermute x6, starting transfers between devices, from_behind(): return lax.ppermute(array, axis, pairs)  88.1 us
    ppermute x31, waiting for transfers between devices, with_halo(): before = lax.ppermute(last, axis, up)  77 us
    ppermute x31, starting transfers between devices, with_halo(): after = lax.ppermute(initial, axis, down)  74.9 us
    another operation x32, loops' own time, guarded(): return lax.cond(segment_live, compute, lambda unused: spare_value, operand)  17.1 us
    dot_general x4, matrix products, forward_local(): coupled = jnp.einsum('rkab,rkbv->rav', blocks, gathered, precision=highest)  16.7 us
  transfers between devices with their start and end apart: 69, of which 37 were waited for; matrix products, arithmetic and copies ran while one was open for 14% of the time, Pallas kernels for 0%

commit v1 on v0

v1 whole, which is shorter than its diff:
```python
from functools import partial

import jax
import jax.numpy as jnp
from jax import lax
from jax.experimental import pallas as pl
from jax.experimental.pallas import tpu as pltpu
from jax.sharding import PartitionSpec as P

B = 64
NV = 16
K = 3
W = 8
LV = 4
RL = 16
ROWS = LV * RL
EXT = RL + 2 * W
VMEM = pltpu.VMEM
SMEM = pltpu.SMEM
F32 = jnp.float32
BF16 = jnp.bfloat16
MIB = 1 << 20


def in_vmem(x):
    return pltpu.with_memory_space_constraint(x, VMEM)


def in_smem(x):
    return pltpu.with_memory_space_constraint(x, SMEM)


def split(x):
    hi = x.astype(BF16)
    lo = (x - hi.astype(F32)).astype(BF16)
    return hi, lo


def nn(a, b):
    return jnp.dot(a, b, preferred_element_type=F32)


def nt(a, b):
    return lax.dot_general(a, b, (((1,), (1,)), ((), ())), preferred_element_type=F32)


def low_half(shape):
    return lax.broadcasted_iota(jnp.int32, shape, len(shape) - 1) % 128 < B


def other_half(x):
    return pltpu.roll(x, B, axis=x.ndim - 1)


def spread_matrix():
    row = lax.broadcasted_iota(jnp.int32, (B * NV, 128), 0) // NV
    col = lax.broadcasted_iota(jnp.int32, (B * NV, 128), 1) % B
    return jnp.where(row == col, 1.0, 0.0).astype(BF16)


def own_lane(rows):
    lane = lax.broadcasted_iota(jnp.int32, (rows, 128), 1) % NV
    vec = lax.broadcasted_iota(jnp.int32, (rows, 128), 0) % NV
    return lane == vec


def state_of_rows(load, count, spread):
    mask = own_lane(NV)
    highs, lows = [], []
    for row in range(count):
        chunks_hi, chunks_lo = [], []
        for chunk in range(B * NV // 128):
            value = jnp.broadcast_to(load(row, chunk), (NV, 128))
            value = jnp.where(mask, value, 0.0)
            hi, lo = split(value)
            chunks_hi.append(hi)
            chunks_lo.append(lo)
        highs.append(jnp.concatenate(chunks_hi, axis=1))
        lows.append(jnp.concatenate(chunks_lo, axis=1))
    out = nn(jnp.concatenate(highs, axis=0), spread) + nn(jnp.concatenate(lows, axis=0), spread)
    return out.reshape(count, NV, 128)


def prep_kernel(index_ref, rhs_ref, lower_hbm, dinv_hbm, w_ref, r_ref, s_ref, low, din, tiles, both, sems):
    def copies(level):
        return (
            pltpu.make_async_copy(lower_hbm.at[level], low.at[level], sems.at[0, level]),
            pltpu.make_async_copy(dinv_hbm.at[level], din.at[level], sems.at[1, level]),
        )

    for level in range(LV):
        for copy in copies(level):
            copy.start()

    def copy_index(i, carry):
        s_ref[i] = index_ref[i]
        return carry

    lax.fori_loop(0, index_ref.shape[0], copy_index, 0)
    spread = spread_matrix()

    def rhs_part(i, carry):
        level, half = i // 2, i % 2
        block = rhs_ref[level, pl.ds(pl.multiple_of(half * 8, 8), 8), :]
        for part in range(2):

            def load(row, chunk):
                return block[part * 4 + row:part * 4 + row + 1, chunk * 128:(chunk + 1) * 128]

            r_ref[pl.ds(i * 8 + part * 4, 4)] = state_of_rows(load, 4, spread)
        return carry

    lax.fori_loop(0, LV * 2, rhs_part, 0)
    left = low_half((B // 2, 128))
    left_wide = low_half((B, 128))

    for level in range(LV):
        for copy in copies(level):
            copy.wait()

        def half_level(half, carry):
            start = pl.multiple_of(half * 8, 8)
            for k in range(K + 1):
                for chunk in range(B * B // 128):
                    lanes = pl.ds(chunk * 128, 128)
                    if k < K:
                        value = low[level, k, pl.ds(start, 8), lanes]
                    else:
                        value = din[level, pl.ds(start, 8), lanes]
                    tiles[k, pl.ds(chunk * 8, 8), :] = value
            for row in range(8):
                part = [tiles[k, pl.ds(row, B // 2, stride=8), :] for k in range(K + 1)]
                turned = [other_half(p) for p in part]
                slot = row % 2
                both[slot, 0, pl.ds(0, B // 2, stride=2), :] = jnp.where(left, part[0], turned[1])
                both[slot, 0, pl.ds(1, B // 2, stride=2), :] = jnp.where(left, turned[0], part[1])
                both[slot, 1, pl.ds(0, B // 2, stride=2), :] = jnp.where(left, part[2], turned[3])
                both[slot, 1, pl.ds(1, B // 2, stride=2), :] = jnp.where(left, turned[2], part[3])
                first, second = both[slot, 0], both[slot, 1]
                diag = other_half(second)[:, :B]
                diag_hi, diag_lo = split(diag)
                right_hi, right_lo = split(jnp.concatenate([first, second], axis=1))
                top = nn(jnp.concatenate([diag_hi, diag_lo], axis=0), right_hi)
                product = top[:B] + top[B:] + nn(diag_hi, right_lo)
                tail = jnp.where(left_wide, product[:, 128:], second)
                hi, lo = split(jnp.concatenate([product[:, :128], tail], axis=1))
                w_ref[level * RL + start + row] = jnp.concatenate([hi, lo], axis=0)
            return carry

        lax.fori_loop(0, 2, half_level, 0)


def adjoint_kernel(index_ref, relayed_ref, a_ref):
    spread = spread_matrix()

    def part(i, carry):
        def load(row, chunk):
            return relayed_ref[index_ref[K * ROWS + i * 4 + row], pl.ds(chunk, 1), :]

        a_ref[pl.ds(i * 4, 4)] = state_of_rows(load, 4, spread)
        return carry

    lax.fori_loop(0, ROWS // 4, part, 0)


def pack(x):
    half = x.shape[0] // 2
    return jnp.where(low_half((half, NV, 128)), x[:half], x[half:])


def unpack(x):
    turned = other_half(x)
    left = low_half(x.shape)
    return jnp.concatenate([jnp.where(left, x, turned), jnp.where(left, turned, x)], axis=0)


FLAGS = (K + 1) * ROWS


def step_kernel(step, cross, turn, s_ref, w_ref, r_ref, a_ref, own_ref, left_ref, right_ref,
                sol_in, adj_in, sol_ref, adj_ref, out_ref, outl_ref, outr_ref, ext, acc0, acc1, acc2):
    del sol_in, adj_in
    section = s_ref[FLAGS]
    even = s_ref[FLAGS + 1] == 0
    half = low_half((NV, 128))

    def incoming(do):
        if own_ref is None:
            return
        if not cross:
            do(left_ref, right_ref)
        else:
            pl.when(even)(lambda: do(right_ref, left_ref))
            pl.when(jnp.logical_not(even))(lambda: do(left_ref, right_ref))

    def outgoing(to_left, to_right):
        if not turn:
            outl_ref[...] = to_left
            outr_ref[...] = to_right
        else:
            @pl.when(even)
            def _():
                outl_ref[...] = to_right
                outr_ref[...] = to_left

            @pl.when(jnp.logical_not(even))
            def _():
                outl_ref[...] = to_left
                outr_ref[...] = to_right

    rnd, t = divmod(step, LV)

    @pl.when(section == rnd)
    def _():
        level = t
        first = step == 0
        if not first:
            ext[pl.ds(W, RL)] = unpack(own_ref[...])

            def fill(from_left, from_right):
                ext[pl.ds(0, W)] = unpack(from_left[...])
                ext[pl.ds(W + RL, W)] = unpack(from_right[...])

            incoming(fill)
        results = []
        for row in range(RL):
            flat = level * RL + row
            source = r_ref[flat]
            if first:
                lhs = jnp.concatenate([jnp.zeros_like(source), jnp.where(half, 0.0, -source)], axis=1)
            else:
                x0, x1, x2 = [ext[s_ref[flat * K + k]] for k in range(K)]
                lhs = jnp.concatenate([jnp.where(half, x0, x1), jnp.where(half, x2, -source)], axis=1)
            hi, lo = split(lhs)
            out = nt(jnp.concatenate([hi, lo], axis=0), w_ref[flat])
            out = out[:NV] + out[NV:]
            out = -(out + other_half(out))
            sol_ref[flat] = out
            results.append(out)
        x = jnp.stack(results)
        out_ref[...] = pack(x)
        outgoing(pack(x[:W]), pack(x[W:]))

    @pl.when(section == LV - 1 - rnd)
    def _():
        level = LV - 1 - t
        first = step == 0
        if not first:
            ext[pl.ds(0, RL)] = unpack(own_ref[...])

            def add(from_left, from_right):
                ext[pl.ds(0, W)] += unpack(from_left[...])
                ext[pl.ds(W, W)] += unpack(from_right[...])

            incoming(add)
        zeros = jnp.zeros((EXT, NV, 128), F32)
        acc0[...] = zeros
        acc1[...] = zeros
        acc2[...] = zeros
        for row in range(RL):
            flat = level * RL + row
            e = a_ref[flat]
            if not first:
                e = e - ext[row]
            hi, lo = split(e)
            out = nn(jnp.concatenate([hi, lo], axis=0), w_ref[flat])
            out = out[:NV] + out[NV:]
            adj_ref[flat] = out[:, 128:]
            i0, i1, i2 = [s_ref[flat * K + k] for k in range(K)]
            acc0[i0] += out[:, :128]
            acc1[i1] += out[:, :128]
            acc2[i2] += out[:, 128:]
        total = jnp.where(low_half((EXT, NV, 128)), acc0[...] + acc2[...], acc1[...])
        total = total + other_half(total)
        out_ref[...] = pack(total[W:W + RL])
        outgoing(pack(total[:W]), pack(total[W + RL:]))


def rows_kernel(x_ref, out_ref):
    spread = jnp.where(low_half((B * NV, 128)), 0.0, spread_matrix().astype(F32)).astype(BF16)
    gather = jnp.where(
        lax.broadcasted_iota(jnp.int32, (RL, RL * NV), 1) // NV
        == lax.broadcasted_iota(jnp.int32, (RL, RL * NV), 0), 1.0, 0.0).astype(BF16)
    mask = own_lane(RL * NV)

    def body(level, carry):
        x = x_ref[pl.ds(level * RL, RL)].reshape(RL * NV, 128)
        parts = split(x)
        for chunk in range(B * NV // 128):
            total = None
            for part in parts:
                wide = nt(part, spread[chunk * 128:(chunk + 1) * 128])
                kept = jnp.where(mask, wide, 0.0).astype(BF16)
                value = nn(gather, kept)
                total = value if total is None else total + value
            out_ref[level, :, pl.ds(chunk * 128, 128)] = total
        return carry

    lax.fori_loop(0, LV, body, 0)


def vspec():
    return pl.BlockSpec(memory_space=VMEM)


def sspec():
    return pl.BlockSpec(memory_space=SMEM)


def hspec():
    return pl.BlockSpec(memory_space=pl.ANY)


STATE = (ROWS, NV, 128)
OWN = (RL // 2, NV, 128)
SIDE = (W // 2, NV, 128)


def prepare(index, rhs, lower, dinv):
    return pl.pallas_call(
        prep_kernel,
        out_shape=(VMEM((ROWS, 2 * B, 256), BF16), VMEM(STATE, F32), SMEM(index.shape, jnp.int32)),
        in_specs=[sspec(), vspec(), hspec(), hspec()],
        out_specs=(vspec(), vspec(), sspec()),
        scratch_shapes=[
            VMEM((LV, K, RL, B * B), F32),
            VMEM((LV, RL, B * B), F32),
            VMEM((K + 1, 8 * B * B // 128, 128), F32),
            VMEM((2, 2, B, 128), F32),
            pltpu.SemaphoreType.DMA((2, LV)),
        ],
        compiler_params=pltpu.CompilerParams(vmem_limit_bytes=24 * MIB),
        name="prepare",
    )(index, in_vmem(rhs), lower, dinv)


def adjoint_state(index, relayed):
    return pl.pallas_call(
        adjoint_kernel,
        out_shape=VMEM(STATE, F32),
        in_specs=[sspec(), vspec()],
        out_specs=vspec(),
        compiler_params=pltpu.CompilerParams(vmem_limit_bytes=16 * MIB),
        name="adjoint_state",
    )(index, in_vmem(relayed))


def run_step(step, index, blocks, source, adjoint, own, left, right, sol, adj):
    turn = step % LV != LV - 1
    cross = step % LV != 0
    has_in = own is not None
    kernel_args = [in_smem(index), in_vmem(blocks), in_vmem(source), in_vmem(adjoint)]
    specs = [sspec(), vspec(), vspec(), vspec()]
    if has_in:
        kernel_args += [in_vmem(own), in_vmem(left), in_vmem(right)]
        specs += [vspec()] * 3
    aliases = {}
    if sol is not None:
        aliases = {len(kernel_args): 0, len(kernel_args) + 1: 1}
        kernel_args += [in_vmem(sol), in_vmem(adj)]
        specs += [vspec()] * 2

    def body(*refs):
        refs = list(refs)
        head, refs = refs[:4], refs[4:]
        arrivals = [None] * 3
        if has_in:
            arrivals, refs = refs[:3], refs[3:]
        held = [None] * 2
        if sol is not None:
            held, refs = refs[:2], refs[2:]
        step_kernel(step, cross, turn, *head, *arrivals, *held, *refs)

    return pl.pallas_call(
        body,
        out_shape=(VMEM(STATE, F32), VMEM(STATE, F32), VMEM(OWN, F32), VMEM(SIDE, F32), VMEM(SIDE, F32)),
        in_specs=specs,
        out_specs=(vspec(),) * 5,
        scratch_shapes=[VMEM((EXT, NV, 128), F32)] * 4,
        input_output_aliases=aliases,
        compiler_params=pltpu.CompilerParams(vmem_limit_bytes=16 * MIB),
        name="step%d" % step,
    )(*kernel_args)


def to_rows(state):
    return pl.pallas_call(
        rows_kernel,
        out_shape=jax.ShapeDtypeStruct((LV, RL, B * NV), F32),
        in_specs=[vspec()],
        out_specs=vspec(),
        compiler_params=pltpu.CompilerParams(vmem_limit_bytes=16 * MIB),
        name="to_rows",
    )(in_vmem(state))


def per_device(rhs, adjoint_owned, owner_of, columns, lower, dinv):
    cells = lax.axis_size("cell")
    sections = lax.axis_size("lvl")
    cell = lax.axis_index("cell")
    section = lax.axis_index("lvl")
    span = RL * cells
    owned = adjoint_owned.reshape(1, cells, B * NV)
    relayed = lax.all_to_all(owned, "cell", split_axis=1, concat_axis=1, tiled=True).reshape(ROWS, B * NV // 128, 128)
    position = cell * RL + jnp.arange(RL, dtype=jnp.int32)
    offset = (columns - position[None, :, None] + span // 2) % span - span // 2
    ext_index = jnp.clip(offset + jnp.arange(RL, dtype=jnp.int32)[None, :, None] + W, 0, EXT - 1)
    owner_row = owner_of % span
    owner_local = owner_of // span % LV * RL + owner_row % RL
    take = owner_local // cells * cells + owner_row // RL
    index = jnp.concatenate([
        ext_index.reshape(-1), take.reshape(-1),
        jnp.stack([section, cell % 2]).astype(jnp.int32),
    ])
    blocks, source, index = prepare(index, rhs, jnp.transpose(lower, (0, 2, 1, 3)), dinv)
    adjoint = adjoint_state(in_smem(index), relayed)

    near = [(i, i ^ 1) for i in range(cells)]
    far = [(i, (i + 1 if i % 2 else i - 1) % cells) for i in range(cells)]

    def handoff(x, rnd, by):
        moves = [(rnd, rnd + 1), (sections - 1 - rnd, sections - 2 - rnd)]
        pairs = [(a * cells + i, b * cells + (i + by) % cells) for a, b in moves for i in range(cells)]
        return lax.ppermute(x, ("lvl", "cell"), pairs)

    own = left = right = sol = adj = None
    for step in range(sections * LV):
        sol, adj, own, left, right = run_step(step, index, blocks, source, adjoint, own, left, right, sol, adj)
        if step == sections * LV - 1:
            break
        if step % LV != LV - 1:
            far_in = lax.ppermute(right, "cell", far)
            near_in = lax.ppermute(left, "cell", near)
            left, right = near_in, far_in
        else:
            rnd = step // LV
            from_right = handoff(left, rnd, -1)
            from_left = handoff(right, rnd, 1)
            own = handoff(own, rnd, 0)
            left, right = from_left, from_right
    return to_rows(sol), to_rows(adj)


def solution(mesh):
    return jax.shard_map(
        per_device,
        mesh=mesh,
        in_specs=(
            P("lvl", "cell", None),
            P("lvl", "cell", None),
            P("lvl", "cell"),
            P("lvl", "cell", None),
            P("lvl", "cell", None, None),
            P("lvl", "cell", None),
        ),
        out_specs=(P("lvl", "cell", None), P("lvl", "cell", None)),
        check_vma=False,
    )
```

time: 777 us -> 182 us (0.23)
  the two profiles are of different devices: /device:TPU:0 before, /device:TPU:24 now
where the time goes in v1:
time: 182 us; the launch traced here: 181 us
  waiting for transfers between devices  76.9 us (42%)
  starting transfers between devices  56.7 us (31%)
  Pallas kernels  34.8 us (19%)
  local copies, waits for them, and re-layouts  10.5 us (6%)
    ppermute x12, waiting for transfers between devices, per_device(): far_in = lax.ppermute(right, 'cell', far)  50 us
    ppermute x12, starting transfers between devices, per_device(): far_in = lax.ppermute(right, 'cell', far)  30.9 us
    ppermute x9, waiting for transfers between devices, handoff(): return lax.ppermute(x, ('lvl', 'cell'), pairs)  26.9 us
    pallas_call x2, Pallas kernels, to_rows(): pl.pallas_call(rows_kernel, out_shape=jax.ShapeDtypeStruct((LV, RL, B * N...  14.9 us
    ppermute x9, starting transfers between devices, handoff(): return lax.ppermute(x, ('lvl', 'cell'), pairs)  12.9 us
    all_to_all x1, starting transfers between devices, per_device(): lax.all_to_all(owned, 'cell', split_axis=1, concat_axis=1, tiled=True)  11.9 us
    pallas_call x1, Pallas kernels, prepare(): pl.pallas_call(prep_kernel, out_shape=(VMEM((ROWS, 2 * B, 256), BF16), VM...  10.5 us
    unnamed x10, local copies, waits for them, and re-layouts  8.22 us
  transfers between devices with their start and end apart: 34, of which 14 were waited for; matrix products, arithmetic and copies ran while one was open for 1% of the time, Pallas kernels for 6%

profile of v1, /device:TPU:24, one launch (start us, length us, event | category | flops | bytes accessed | tf_op | source)
XLA Modules:
  0.0 181.3 jit_solution(18386496198150805887)
XLA Ops:
  2.6 11.9 %all-to-all-start = ((f32[1,64,1024]{2,0,1:T(1,128)}), f32[1,64,1024]{2,0,1:T(1,128)S(1)}, u32[]{:S(2)}, u32[]{:S(2)}) async-start(f32[1,64,1024]{2,0,1:T(1,128)} %reshape.22), calls=%async_computation | async-start | bytes 524288 | tf_op jit(solution)/shard_map/all_to_all | solution.py:404
  20.4 10.5 %prepare.1 = (bf16[64,128,256]{2,1,0:T(8,128)(2,1)S(1)}, f32[64,16,128]{2,1,0:T(8,128)S(1)}, s32[258]{0:T(512)S(4)}) custom-call(s32[258]{0:T(512)S(1)} %pad_add_fusion.index_ref, f32[4,16,1024]{2,1,0:T(8,128)S(1)} %copy-done.4, f32[4,3,16,4096]{3,2,1,0:T(8,128)S(1)} %bitcast.4, f32[4,16,4096]{2,1,0:T(8,128)S(1)} %copy-done.3), custom_call_target="tpu_custom_call" | custom-call | tf_op jit(solution)/shard_map/prepare/pallas_call | solution.py:320
  30.9 2.0 %copy-done = bf16[64,128,256]{2,1,0:T(8,128)(2,1)} copy-done((bf16[64,128,256]{2,1,0:T(8,128)(2,1)}, bf16[64,128,256]{2,1,0:T(8,128)(2,1)S(1)}, u32[]{:S(2)}) %copy-start) | copy-done | bytes 4194328
  32.9 4.0 %adjoint_state.1.refs_3_ = f32[64,16,128]{2,1,0:T(8,128)S(1)} custom-call(s32[258]{0:T(512)S(4)} %get-tuple-element.82.index_ref.refs_0_, f32[64,8,128]{2,1,0:T(8,128)S(1)} %bitcast.5), custom_call_target="tpu_custom_call" | custom-call | tf_op jit(solution)/shard_map/adjoint_state/pallas_call | solution.py:338
  37.0 2.2 %copy-done.1 = bf16[64,128,256]{2,1,0:T(8,128)(2,1)S(1)} copy-done((bf16[64,128,256]{2,1,0:T(8,128)(2,1)S(1)}, bf16[64,128,256]{2,1,0:T(8,128)(2,1)}, u32[]{:S(2)}) %copy-start.1) | copy-done | bytes 4194328
  39.7 5.3 %collective-permute-start.1 = (f32[4,16,128]{2,1,0:T(8,128)S(1)}, f32[4,16,128]{2,1,0:T(8,128)S(1)}, u32[]{:S(2)}, u32[]{:S(2)}) collective-permute-start(f32[4,16,128]{2,1,0:T(8,128)S(1)} %get-tuple-element.87), channel_id=1, source_target_pairs={{0,63},{1,2},{2,1},{3,4},{4,3},{5,6},{6,5},{7,8},{8,7},{9,10},{10,... | collective-permute-start | bytes 98312 | tf_op jit(solution)/shard_map/ppermute | solution.py:432
  47.2 5.2 %collective-permute-start.3 = (f32[4,16,128]{2,1,0:T(8,128)S(1)}, f32[4,16,128]{2,1,0:T(8,128)S(1)}, u32[]{:S(2)}, u32[]{:S(2)}) collective-permute-start(f32[4,16,128]{2,1,0:T(8,128)S(1)} %get-tuple-element.92), channel_id=1, source_target_pairs={{0,63},{1,2},{2,1},{3,4},{4,3},{5,6},{6,5},{7,8},{8,7},{9,10},{10,... | collective-permute-start | bytes 98312 | tf_op jit(solution)/shard_map/ppermute | solution.py:432
  54.7 5.2 %collective-permute-start.5 = (f32[4,16,128]{2,1,0:T(8,128)S(1)}, f32[4,16,128]{2,1,0:T(8,128)S(1)}, u32[]{:S(2)}, u32[]{:S(2)}) collective-permute-start(f32[4,16,128]{2,1,0:T(8,128)S(1)} %get-tuple-element.97), channel_id=1, source_target_pairs={{0,63},{1,2},{2,1},{3,4},{4,3},{5,6},{6,5},{7,8},{8,7},{9,10},{10,... | collective-permute-start | bytes 98312 | tf_op jit(solution)/shard_map/ppermute | solution.py:432
  64.7 4.5 %collective-permute-start.8 = (f32[4,16,128]{2,1,0:T(8,128)S(1)}, f32[4,16,128]{2,1,0:T(8,128)S(1)}, u32[]{:S(2)}, u32[]{:S(2)}) collective-permute-start(f32[4,16,128]{2,1,0:T(8,128)S(1)} %get-tuple-element.102), channel_id=1, source_target_pairs={{0,127},{1,64},{2,65},{3,66},{4,67},{5,68},{6,69},{7,70},{8,71},{9... | collective-permute-start | bytes 98312 | tf_op jit(solution)/shard_map/ppermute | solution.py:424
  72.3 5.3 %collective-permute-done.10.refs_6_ = f32[4,16,128]{2,1,0:T(8,128)S(1)} collective-permute-done((f32[4,16,128]{2,1,0:T(8,128)S(1)}, f32[4,16,128]{2,1,0:T(8,128)S(1)}, u32[]{:S(2)}, u32[]{:S(2)}) %collective-permute-start.10) | collective-permute-done | bytes 32800 | tf_op jit(solution)/shard_map/ppermute | solution.py:432
  79.0 5.3 %collective-permute-done.12.refs_6_ = f32[4,16,128]{2,1,0:T(8,128)S(1)} collective-permute-done((f32[4,16,128]{2,1,0:T(8,128)S(1)}, f32[4,16,128]{2,1,0:T(8,128)S(1)}, u32[]{:S(2)}, u32[]{:S(2)}) %collective-permute-start.12) | collective-permute-done | bytes 32800 | tf_op jit(solution)/shard_map/ppermute | solution.py:432
  85.6 5.3 %collective-permute-done.14.refs_6_ = f32[4,16,128]{2,1,0:T(8,128)S(1)} collective-permute-done((f32[4,16,128]{2,1,0:T(8,128)S(1)}, f32[4,16,128]{2,1,0:T(8,128)S(1)}, u32[]{:S(2)}, u32[]{:S(2)}) %collective-permute-start.14) | collective-permute-done | bytes 32800 | tf_op jit(solution)/shard_map/ppermute | solution.py:432
  94.6 5.3 %collective-permute-done.19.refs_6_ = f32[4,16,128]{2,1,0:T(8,128)S(1)} collective-permute-done((f32[4,16,128]{2,1,0:T(8,128)S(1)}, f32[4,16,128]{2,1,0:T(8,128)S(1)}, u32[]{:S(2)}, u32[]{:S(2)}) %collective-permute-start.19) | collective-permute-done | bytes 32800 | tf_op jit(solution)/shard_map/ppermute | solution.py:432
  101.2 5.3 %collective-permute-done.21.refs_6_ = f32[4,16,128]{2,1,0:T(8,128)S(1)} collective-permute-done((f32[4,16,128]{2,1,0:T(8,128)S(1)}, f32[4,16,128]{2,1,0:T(8,128)S(1)}, u32[]{:S(2)}, u32[]{:S(2)}) %collective-permute-start.21) | collective-permute-done | bytes 32800 | tf_op jit(solution)/shard_map/ppermute | solution.py:432
  107.9 5.3 %collective-permute-done.23.refs_6_ = f32[4,16,128]{2,1,0:T(8,128)S(1)} collective-permute-done((f32[4,16,128]{2,1,0:T(8,128)S(1)}, f32[4,16,128]{2,1,0:T(8,128)S(1)}, u32[]{:S(2)}, u32[]{:S(2)}) %collective-permute-start.23) | collective-permute-done | bytes 32800 | tf_op jit(solution)/shard_map/ppermute | solution.py:432
  117.1 25.3 %collective-permute-done.25.refs_5_ = f32[4,16,128]{2,1,0:T(8,128)S(1)} collective-permute-done((f32[4,16,128]{2,1,0:T(8,128)S(1)}, f32[4,16,128]{2,1,0:T(8,128)S(1)}, u32[]{:S(2)}, u32[]{:S(2)}) %collective-permute-start.25) | collective-permute-done | bytes 32800 | tf_op jit(solution)/shard_map/ppermute | solution.py:424
  143.3 2.3 %collective-permute-start.28 = (f32[4,16,128]{2,1,0:T(8,128)S(1)}, f32[4,16,128]{2,1,0:T(8,128)S(1)}, u32[]{:S(2)}, u32[]{:S(2)}) collective-permute-start(f32[4,16,128]{2,1,0:T(8,128)S(1)} %get-tuple-element.147), channel_id=1, source_target_pairs={{0,63},{1,2},{2,1},{3,4},{4,3},{5,6},{6,5},{7,8},{8,7},{9,10},{10,... | collective-permute-start | bytes 98312 | tf_op jit(solution)/shard_map/ppermute | solution.py:432
  145.6 4.4 %collective-permute-done.28.refs_6_ = f32[4,16,128]{2,1,0:T(8,128)S(1)} collective-permute-done((f32[4,16,128]{2,1,0:T(8,128)S(1)}, f32[4,16,128]{2,1,0:T(8,128)S(1)}, u32[]{:S(2)}, u32[]{:S(2)}) %collective-permute-start.28) | collective-permute-done | bytes 32800 | tf_op jit(solution)/shard_map/ppermute | solution.py:432
  150.8 2.3 %collective-permute-start.30 = (f32[4,16,128]{2,1,0:T(8,128)S(1)}, f32[4,16,128]{2,1,0:T(8,128)S(1)}, u32[]{:S(2)}, u32[]{:S(2)}) collective-permute-start(f32[4,16,128]{2,1,0:T(8,128)S(1)} %get-tuple-element.152), channel_id=1, source_target_pairs={{0,63},{1,2},{2,1},{3,4},{4,3},{5,6},{6,5},{7,8},{8,7},{9,10},{10,... | collective-permute-start | bytes 98312 | tf_op jit(solution)/shard_map/ppermute | solution.py:432
  153.2 4.4 %collective-permute-done.30.refs_6_ = f32[4,16,128]{2,1,0:T(8,128)S(1)} collective-permute-done((f32[4,16,128]{2,1,0:T(8,128)S(1)}, f32[4,16,128]{2,1,0:T(8,128)S(1)}, u32[]{:S(2)}, u32[]{:S(2)}) %collective-permute-start.30) | collective-permute-done | bytes 32800 | tf_op jit(solution)/shard_map/ppermute | solution.py:432
  158.3 2.4 %collective-permute-start.32 = (f32[4,16,128]{2,1,0:T(8,128)S(1)}, f32[4,16,128]{2,1,0:T(8,128)S(1)}, u32[]{:S(2)}, u32[]{:S(2)}) collective-permute-start(f32[4,16,128]{2,1,0:T(8,128)S(1)} %get-tuple-element.157), channel_id=1, source_target_pairs={{0,63},{1,2},{2,1},{3,4},{4,3},{5,6},{6,5},{7,8},{8,7},{9,10},{10,... | collective-permute-start | bytes 98312 | tf_op jit(solution)/shard_map/ppermute | solution.py:432
  160.7 4.4 %collective-permute-done.32.refs_6_ = f32[4,16,128]{2,1,0:T(8,128)S(1)} collective-permute-done((f32[4,16,128]{2,1,0:T(8,128)S(1)}, f32[4,16,128]{2,1,0:T(8,128)S(1)}, u32[]{:S(2)}, u32[]{:S(2)}) %collective-permute-start.32) | collective-permute-done | bytes 32800 | tf_op jit(solution)/shard_map/ppermute | solution.py:432
  166.4 7.5 %to_rows.2 = f32[4,16,1024]{2,1,0:T(8,128)} custom-call(f32[64,16,128]{2,1,0:T(8,128)S(1)} %get-tuple-element.160.x_ref), custom_call_target="tpu_custom_call" | custom-call | tf_op jit(solution)/shard_map/to_rows/pallas_call | solution.py:387
  173.8 7.5 %to_rows.3 = f32[4,16,1024]{2,1,0:T(8,128)} custom-call(f32[64,16,128]{2,1,0:T(8,128)S(1)} %get-tuple-element.161.x_ref), custom_call_target="tpu_custom_call" | custom-call | tf_op jit(solution)/shard_map/to_rows/pallas_call | solution.py:387
  (82 shorter events, 37.3 us)
Async XLA Ops:
  2.6 30.3 %all-to-all-start = ((f32[1,64,1024]{2,0,1:T(1,128)}), f32[1,64,1024]{2,0,1:T(1,128)S(1)}, u32[]{:S(2)}, u32[]{:S(2)}) async-start(f32[1,64,1024]{2,0,1:T(1,128)} %reshape.22), calls=%async_computation | async-start | bytes 524288 | tf_op jit(solution)/shard_map/all_to_all | solution.py:404
  39.6 5.4 %collective-permute-start = (f32[4,16,128]{2,1,0:T(8,128)S(1)}, f32[4,16,128]{2,1,0:T(8,128)S(1)}, u32[]{:S(2)}, u32[]{:S(2)}) collective-permute-start(f32[4,16,128]{2,1,0:T(8,128)S(1)} %get-tuple-element.86), channel_id=1, source_target_pairs={{0,1},{1,0},{2,3},{3,2},{4,5},{5,4},{6,7},{7,6},{8,9},{9,8},{10,11... | collective-permute-start | bytes 98312 | tf_op jit(solution)/shard_map/ppermute | solution.py:433
  39.7 6.9 %collective-permute-start.1 = (f32[4,16,128]{2,1,0:T(8,128)S(1)}, f32[4,16,128]{2,1,0:T(8,128)S(1)}, u32[]{:S(2)}, u32[]{:S(2)}) collective-permute-start(f32[4,16,128]{2,1,0:T(8,128)S(1)} %get-tuple-element.87), channel_id=1, source_target_pairs={{0,63},{1,2},{2,1},{3,4},{4,3},{5,6},{6,5},{7,8},{8,7},{9,10},{10,... | collective-permute-start | bytes 98312 | tf_op jit(solution)/shard_map/ppermute | solution.py:432
  47.1 5.3 %collective-permute-start.2 = (f32[4,16,128]{2,1,0:T(8,128)S(1)}, f32[4,16,128]{2,1,0:T(8,128)S(1)}, u32[]{:S(2)}, u32[]{:S(2)}) collective-permute-start(f32[4,16,128]{2,1,0:T(8,128)S(1)} %get-tuple-element.91), channel_id=1, source_target_pairs={{0,1},{1,0},{2,3},{3,2},{4,5},{5,4},{6,7},{7,6},{8,9},{9,8},{10,11... | collective-permute-start | bytes 98312 | tf_op jit(solution)/shard_map/ppermute | solution.py:433
  47.2 6.8 %collective-permute-start.3 = (f32[4,16,128]{2,1,0:T(8,128)S(1)}, f32[4,16,128]{2,1,0:T(8,128)S(1)}, u32[]{:S(2)}, u32[]{:S(2)}) collective-permute-start(f32[4,16,128]{2,1,0:T(8,128)S(1)} %get-tuple-element.92), channel_id=1, source_target_pairs={{0,63},{1,2},{2,1},{3,4},{4,3},{5,6},{6,5},{7,8},{8,7},{9,10},{10,... | collective-permute-start | bytes 98312 | tf_op jit(solution)/shard_map/ppermute | solution.py:432
  54.6 5.3 %collective-permute-start.4 = (f32[4,16,128]{2,1,0:T(8,128)S(1)}, f32[4,16,128]{2,1,0:T(8,128)S(1)}, u32[]{:S(2)}, u32[]{:S(2)}) collective-permute-start(f32[4,16,128]{2,1,0:T(8,128)S(1)} %get-tuple-element.96), channel_id=1, source_target_pairs={{0,1},{1,0},{2,3},{3,2},{4,5},{5,4},{6,7},{7,6},{8,9},{9,8},{10,11... | collective-permute-start | bytes 98312 | tf_op jit(solution)/shard_map/ppermute | solution.py:433
  54.7 6.8 %collective-permute-start.5 = (f32[4,16,128]{2,1,0:T(8,128)S(1)}, f32[4,16,128]{2,1,0:T(8,128)S(1)}, u32[]{:S(2)}, u32[]{:S(2)}) collective-permute-start(f32[4,16,128]{2,1,0:T(8,128)S(1)} %get-tuple-element.97), channel_id=1, source_target_pairs={{0,63},{1,2},{2,1},{3,4},{4,3},{5,6},{6,5},{7,8},{8,7},{9,10},{10,... | collective-permute-start | bytes 98312 | tf_op jit(solution)/shard_map/ppermute | solution.py:432
  62.1 8.6 %collective-permute-start.6 = (f32[8,16,128]{2,1,0:T(8,128)S(1)}, f32[8,16,128]{2,1,0:T(8,128)S(1)}, u32[]{:S(2)}, u32[]{:S(2)}) collective-permute-start(f32[8,16,128]{2,1,0:T(8,128)S(1)} %get-tuple-element.100), channel_id=1, source_target_pairs={{0,64},{1,65},{2,66},{3,67},{4,68},{5,69},{6,70},{7,71},{8,72},{9,... | collective-permute-start | bytes 196616 | tf_op jit(solution)/shard_map/ppermute | solution.py:424
  63.4 5.8 %collective-permute-start.7 = (f32[4,16,128]{2,1,0:T(8,128)S(1)}, f32[4,16,128]{2,1,0:T(8,128)S(1)}, u32[]{:S(2)}, u32[]{:S(2)}) collective-permute-start(f32[4,16,128]{2,1,0:T(8,128)S(1)} %get-tuple-element.101), channel_id=1, source_target_pairs={{0,65},{1,66},{2,67},{3,68},{4,69},{5,70},{6,71},{7,72},{8,73},{9,... | collective-permute-start | bytes 98312 | tf_op jit(solution)/shard_map/ppermute | solution.py:424
  64.7 6.0 %collective-permute-start.8 = (f32[4,16,128]{2,1,0:T(8,128)S(1)}, f32[4,16,128]{2,1,0:T(8,128)S(1)}, u32[]{:S(2)}, u32[]{:S(2)}) collective-permute-start(f32[4,16,128]{2,1,0:T(8,128)S(1)} %get-tuple-element.102), channel_id=1, source_target_pairs={{0,127},{1,64},{2,65},{3,66},{4,67},{5,68},{6,69},{7,70},{8,71},{9... | collective-permute-start | bytes 98312 | tf_op jit(solution)/shard_map/ppermute | solution.py:424
  70.7 6.9 %collective-permute-start.10 = (f32[4,16,128]{2,1,0:T(8,128)S(1)}, f32[4,16,128]{2,1,0:T(8,128)S(1)}, u32[]{:S(2)}, u32[]{:S(2)}) collective-permute-start(f32[4,16,128]{2,1,0:T(8,128)S(1)} %get-tuple-element.107), channel_id=1, source_target_pairs={{0,63},{1,2},{2,1},{3,4},{4,3},{5,6},{6,5},{7,8},{8,7},{9,10},{10,... | collective-permute-start | bytes 98312 | tf_op jit(solution)/shard_map/ppermute | solution.py:432
  77.7 6.7 %collective-permute-start.12 = (f32[4,16,128]{2,1,0:T(8,128)S(1)}, f32[4,16,128]{2,1,0:T(8,128)S(1)}, u32[]{:S(2)}, u32[]{:S(2)}) collective-permute-start(f32[4,16,128]{2,1,0:T(8,128)S(1)} %get-tuple-element.112), channel_id=1, source_target_pairs={{0,63},{1,2},{2,1},{3,4},{4,3},{5,6},{6,5},{7,8},{8,7},{9,10},{10,... | collective-permute-start | bytes 98312 | tf_op jit(solution)/shard_map/ppermute | solution.py:432
  84.3 6.7 %collective-permute-start.14 = (f32[4,16,128]{2,1,0:T(8,128)S(1)}, f32[4,16,128]{2,1,0:T(8,128)S(1)}, u32[]{:S(2)}, u32[]{:S(2)}) collective-permute-start(f32[4,16,128]{2,1,0:T(8,128)S(1)} %get-tuple-element.117), channel_id=1, source_target_pairs={{0,63},{1,2},{2,1},{3,4},{4,3},{5,6},{6,5},{7,8},{8,7},{9,10},{10,... | collective-permute-start | bytes 98312 | tf_op jit(solution)/shard_map/ppermute | solution.py:432
  93.1 6.7 %collective-permute-start.19 = (f32[4,16,128]{2,1,0:T(8,128)S(1)}, f32[4,16,128]{2,1,0:T(8,128)S(1)}, u32[]{:S(2)}, u32[]{:S(2)}) collective-permute-start(f32[4,16,128]{2,1,0:T(8,128)S(1)} %get-tuple-element.127), channel_id=1, source_target_pairs={{0,63},{1,2},{2,1},{3,4},{4,3},{5,6},{6,5},{7,8},{8,7},{9,10},{10,... | collective-permute-start | bytes 98312 | tf_op jit(solution)/shard_map/ppermute | solution.py:432
  99.9 6.7 %collective-permute-start.21 = (f32[4,16,128]{2,1,0:T(8,128)S(1)}, f32[4,16,128]{2,1,0:T(8,128)S(1)}, u32[]{:S(2)}, u32[]{:S(2)}) collective-permute-start(f32[4,16,128]{2,1,0:T(8,128)S(1)} %get-tuple-element.132), channel_id=1, source_target_pairs={{0,63},{1,2},{2,1},{3,4},{4,3},{5,6},{6,5},{7,8},{8,7},{9,10},{10,... | collective-permute-start | bytes 98312 | tf_op jit(solution)/shard_map/ppermute | solution.py:432
  106.6 6.7 %collective-permute-start.23 = (f32[4,16,128]{2,1,0:T(8,128)S(1)}, f32[4,16,128]{2,1,0:T(8,128)S(1)}, u32[]{:S(2)}, u32[]{:S(2)}) collective-permute-start(f32[4,16,128]{2,1,0:T(8,128)S(1)} %get-tuple-element.137), channel_id=1, source_target_pairs={{0,63},{1,2},{2,1},{3,4},{4,3},{5,6},{6,5},{7,8},{8,7},{9,10},{10,... | collective-permute-start | bytes 98312 | tf_op jit(solution)/shard_map/ppermute | solution.py:432
  113.2 29.2 %collective-permute-start.24 = (f32[8,16,128]{2,1,0:T(8,128)S(1)}, f32[8,16,128]{2,1,0:T(8,128)S(1)}, u32[]{:S(2)}, u32[]{:S(2)}) collective-permute-start(f32[8,16,128]{2,1,0:T(8,128)S(1)} %get-tuple-element.140), channel_id=1, source_target_pairs={{128,192},{129,193},{130,194},{131,195},{132,196},{133,197},{134,1... | collective-permute-start | bytes 196616 | tf_op jit(solution)/shard_map/ppermute | solution.py:424
  114.5 27.9 %collective-permute-start.25 = (f32[4,16,128]{2,1,0:T(8,128)S(1)}, f32[4,16,128]{2,1,0:T(8,128)S(1)}, u32[]{:S(2)}, u32[]{:S(2)}) collective-permute-start(f32[4,16,128]{2,1,0:T(8,128)S(1)} %get-tuple-element.141), channel_id=1, source_target_pairs={{128,193},{129,194},{130,195},{131,196},{132,197},{133,198},{134,1... | collective-permute-start | bytes 98312 | tf_op jit(solution)/shard_map/ppermute | solution.py:424
  115.8 26.6 %collective-permute-start.26 = (f32[4,16,128]{2,1,0:T(8,128)S(1)}, f32[4,16,128]{2,1,0:T(8,128)S(1)}, u32[]{:S(2)}, u32[]{:S(2)}) collective-permute-start(f32[4,16,128]{2,1,0:T(8,128)S(1)} %get-tuple-element.142), channel_id=1, source_target_pairs={{128,255},{129,192},{130,193},{131,194},{132,195},{133,196},{134,1... | collective-permute-start | bytes 98312 | tf_op jit(solution)/shard_map/ppermute | solution.py:424
  143.0 2.6 %collective-permute-start.27 = (f32[4,16,128]{2,1,0:T(8,128)S(1)}, f32[4,16,128]{2,1,0:T(8,128)S(1)}, u32[]{:S(2)}, u32[]{:S(2)}) collective-permute-start(f32[4,16,128]{2,1,0:T(8,128)S(1)} %get-tuple-element.146), channel_id=1, source_target_pairs={{0,1},{1,0},{2,3},{3,2},{4,5},{5,4},{6,7},{7,6},{8,9},{9,8},{10,11... | collective-permute-start | bytes 98312 | tf_op jit(solution)/shard_map/ppermute | solution.py:433
  143.3 6.7 %collective-permute-start.28 = (f32[4,16,128]{2,1,0:T(8,128)S(1)}, f32[4,16,128]{2,1,0:T(8,128)S(1)}, u32[]{:S(2)}, u32[]{:S(2)}) collective-permute-start(f32[4,16,128]{2,1,0:T(8,128)S(1)} %get-tuple-element.147), channel_id=1, source_target_pairs={{0,63},{1,2},{2,1},{3,4},{4,3},{5,6},{6,5},{7,8},{8,7},{9,10},{10,... | collective-permute-start | bytes 98312 | tf_op jit(solution)/shard_map/ppermute | solution.py:432
  150.8 6.7 %collective-permute-start.30 = (f32[4,16,128]{2,1,0:T(8,128)S(1)}, f32[4,16,128]{2,1,0:T(8,128)S(1)}, u32[]{:S(2)}, u32[]{:S(2)}) collective-permute-start(f32[4,16,128]{2,1,0:T(8,128)S(1)} %get-tuple-element.152), channel_id=1, source_target_pairs={{0,63},{1,2},{2,1},{3,4},{4,3},{5,6},{6,5},{7,8},{8,7},{9,10},{10,... | collective-permute-start | bytes 98312 | tf_op jit(solution)/shard_map/ppermute | solution.py:432
  158.2 2.5 %collective-permute-start.31 = (f32[4,16,128]{2,1,0:T(8,128)S(1)}, f32[4,16,128]{2,1,0:T(8,128)S(1)}, u32[]{:S(2)}, u32[]{:S(2)}) collective-permute-start(f32[4,16,128]{2,1,0:T(8,128)S(1)} %get-tuple-element.156), channel_id=1, source_target_pairs={{0,1},{1,0},{2,3},{3,2},{4,5},{5,4},{6,7},{7,6},{8,9},{9,8},{10,11... | collective-permute-start | bytes 98312 | tf_op jit(solution)/shard_map/ppermute | solution.py:433
  158.3 6.7 %collective-permute-start.32 = (f32[4,16,128]{2,1,0:T(8,128)S(1)}, f32[4,16,128]{2,1,0:T(8,128)S(1)}, u32[]{:S(2)}, u32[]{:S(2)}) collective-permute-start(f32[4,16,128]{2,1,0:T(8,128)S(1)} %get-tuple-element.157), channel_id=1, source_target_pairs={{0,63},{1,2},{2,1},{3,4},{4,3},{5,6},{6,5},{7,8},{8,7},{9,10},{10,... | collective-permute-start | bytes 98312 | tf_op jit(solution)/shard_map/ppermute | solution.py:432
  (15 other events, 23.2 us)
